TPU v7x, 32 devices: a whole 2x2x4 slice. The times are simulated.
32 devices in a mesh: user: 4 (over y, x), item: 8 (over z, core).
Axes of the slice: x: 2, y: 2, z: 4, core: 2. Of those that a mesh axis runs over, the one named last changes fastest.
Arguments:
- user_cot: bfloat16 [6144, 64], P(('user', 'item')), may hold values from -6 to 6
- item_cot: bfloat16 [16384, 64], P(('item', 'user')), may hold values from -6 to 6
- tile_weight: int32 [64, 2048, 256], P('user', 'item'), may hold values from 0 to 3
- tile_rows: int32 [4, 128], P('user', 'item'), may hold values from 0 to 5, as said below
- tile_cols: int32 [4, 128], P('user', 'item'), may hold values from 0 to 7, as said below
- tile_count: int32 [4, 8], P('user', 'item'), may hold values from 4 to 16, as said below
- user_degree: int32 [6144], P('user'), may hold values from 35 to 139
- item_degree: int32 [16384], P('item'), may hold values from 48 to 191
Outputs:
- user_grad: bfloat16 [6144, 64], P(('user', 'item'))
- item_grad: bfloat16 [16384, 64], P(('item', 'user'))
Inputs may be any that keep to these rules, and one draw needn't show every extreme that they name: `tile_rows`: entries past a device's count are padding. Among a device's live slots no (row, column) pair repeats. `tile_cols`: paired with tile_rows slot by slot. `tile_count`: some device holds 16 live slots.
All inputs are finite; a program needn't handle non-finite values.
Results may differ from a plain program's by a relative error of at most 0.0034.
Values may be sent and summed in bfloat16 or wider, within the bound.
A program may use at most 64 MiB of HBM per device.

v0:
```python
import jax
import jax.numpy as jnp
from jax import lax
from jax.sharding import PartitionSpec as P


def build_tiles(weights, row_ids, col_ids, live_count, user_deg, item_deg):
    tile_slots, tile_size = (weights.shape[0], weights.shape[2])
    row_scale = lax.rsqrt(user_deg.astype(jnp.float32)).reshape(-1, tile_size)
    col_scale = lax.rsqrt(item_deg.astype(jnp.float32)).reshape(-1, tile_size)
    row_onehot = (
        row_ids[:, None] == jnp.arange(row_scale.shape[0], dtype=jnp.int32)[None, :]
    ).astype(jnp.float32)
    col_onehot = (
        col_ids[:, None] == jnp.arange(col_scale.shape[0], dtype=jnp.int32)[None, :]
    ).astype(jnp.float32)
    live_mask = (jnp.arange(tile_slots, dtype=jnp.int32) < live_count).astype(jnp.float32)
    row_factor = (
        jnp.dot(row_onehot, row_scale, precision=lax.Precision.HIGHEST) * live_mask[:, None]
    )
    col_factor = jnp.dot(col_onehot, col_scale, precision=lax.Precision.HIGHEST)
    adjacency = (
        weights.astype(jnp.float32) * row_factor[:, :, None] * col_factor[:, None, :]
    ).astype(jnp.bfloat16)
    return (adjacency, row_onehot, col_onehot)


def toward_items(adjacency, col_onehot, row_ids, user_rows):
    tile_size = adjacency.shape[1]
    panel = user_rows.reshape(-1, tile_size, user_rows.shape[1])
    blocks = jnp.take(panel, row_ids, axis=0)
    contrib = jnp.einsum("trc,trd->tcd", adjacency, blocks, preferred_element_type=jnp.float32)
    summed = jnp.einsum("tb,tcd->bcd", col_onehot, contrib, precision=lax.Precision.HIGHEST)
    return summed.reshape(-1, user_rows.shape[1])


def toward_users(adjacency, row_onehot, col_ids, item_rows):
    tile_size = adjacency.shape[1]
    panel = item_rows.reshape(-1, tile_size, item_rows.shape[1])
    blocks = jnp.take(panel, col_ids, axis=0)
    contrib = jnp.einsum("trc,tcd->trd", adjacency, blocks, preferred_element_type=jnp.float32)
    summed = jnp.einsum("tb,trd->brd", row_onehot, contrib, precision=lax.Precision.HIGHEST)
    return summed.reshape(-1, item_rows.shape[1])


def spread_users(piece):
    return lax.all_gather(piece, "item", axis=0, tiled=True)


def spread_items(piece):
    return lax.all_gather(piece, "user", axis=0, tiled=True)


def settle_items(terms):
    return lax.psum_scatter(terms, "user", scatter_dimension=0, tiled=True)


def settle_users(terms):
    return lax.psum_scatter(terms, "item", scatter_dimension=0, tiled=True)


def shards(
    user_cot, item_cot, tile_weight, tile_rows, tile_cols, tile_count, user_degree, item_degree
):
    row_ids = tile_rows[0]
    col_ids = tile_cols[0]
    adjacency, row_onehot, col_onehot = build_tiles(
        tile_weight, row_ids, col_ids, tile_count[0, 0], user_degree, item_degree
    )
    item_terms = toward_items(adjacency, col_onehot, row_ids, spread_users(user_cot))
    user_terms = toward_users(adjacency, row_onehot, col_ids, spread_items(item_cot))
    once_item = settle_items(item_terms).astype(jnp.bfloat16)
    item_full = spread_items(once_item)
    once_user = settle_users(user_terms).astype(jnp.bfloat16)
    user_full = spread_users(once_user)
    twice_item = settle_items(toward_items(adjacency, col_onehot, row_ids, user_full))
    twice_user = settle_users(toward_users(adjacency, row_onehot, col_ids, item_full))
    user_grad = (
        (user_cot.astype(jnp.float32) + once_user.astype(jnp.float32) + twice_user) / 3.0
    ).astype(jnp.bfloat16)
    item_grad = (
        (item_cot.astype(jnp.float32) + once_item.astype(jnp.float32) + twice_item) / 3.0
    ).astype(jnp.bfloat16)
    return (user_grad, item_grad)


def solution(mesh):
    return jax.shard_map(
        shards,
        mesh=mesh,
        in_specs=(
            P(("user", "item"), None),
            P(("item", "user"), None),
            P("user", "item", None),
            P("user", "item"),
            P("user", "item"),
            P("user", "item"),
            P("user"),
            P("item"),
        ),
        out_specs=(P(("user", "item"), None), P(("item", "user"), None)),
        check_vma=False,
    )
```

profile of v0, /device:TPU:0, one launch (start us, length us, event | category | flops | bytes accessed | tf_op | source)
XLA Modules:
  0.0 169.2 jit_solution(15301617470116322912)
XLA Ops:
  7.2 0.0 copy-start.3
  7.2 0.0 reduce-scatter.13.cloned.1.call-start
  7.2 0.7 compare_select_fusion.1
  7.9 0.7 compare_and_fusion.1
  8.5 0.7 convert_rsqrt_fusion.1
  9.9 0.7 convert_rsqrt_fusion
  10.6 10.7 %all_gather.12 = bf16[2048,64]{0,1:T(8,128)(2,1)S(1)} all-gather(bf16[512,64]{0,1:T(8,128)(2,1)} %param.13), channel_id=1, replica_groups=mesh['user'=4,'item'=8] {'user'}, dimensions={0}, use_global_device_ids=true | all-gather | bytes 327680 | tf_op jit(solution)/shard_map/all_gather | solution.py:51
  21.4 0.8 fusion.25
  22.2 0.6 gather_fusion
  22.8 0.0 copy-done.3
  22.8 0.2 convolution_multiply_fusion
  23.0 2.6 %multiply_convert_fusion = bf16[16,256,256]{2,1,0:T(8,128)(2,1)S(1)} fusion(s32[16,256,256]{2,1,0:T(8,128)} %param.14, f32[16,256]{1,0:T(8,128)S(1)} %fusion.25, f32[16,256]{1,0:T(8,128)S(1)} %convolution_multiply_fusion), kind=kLoop, calls=%fused_computation.4 | loop fusion | flops 4194304 | bytes 6324224 | tf_op jit(solution)/shard_map/convert_element_type | solution.py:24
  25.6 0.8 fusion.14
  26.4 0.0 copy-start.1
  26.4 1.1 fusion.6
  27.5 1.2 copy.36
  28.7 0.0 reduce-scatter.13.cloned.1.call-update
  28.7 0.0 reduce-scatter.9.cloned.1.call-start
  28.8 0.0 copy-done.1
  28.8 14.6 %all-gather = bf16[8,192,64]{1,2,0:T(8,128)(2,1)S(1)} all-gather(bf16[1,192,64]{1,2,0:T(8,128)(2,1)S(1)} %bitcast.63), channel_id=1, replica_groups=mesh['user'=4,'item'=8] {'item'}, dimensions={0}, use_global_device_ids=true | all-gather | bytes 221184 | tf_op jit(solution)/shard_map/all_gather | solution.py:47
  43.4 0.1 copy.24
  43.6 0.3 reshape.57
  44.0 0.6 gather_fusion.1
  44.5 0.0 copy-start.2
  44.6 0.5 fusion.12
  45.1 0.1 copy-done.2
  45.2 1.1 fusion.4
  46.3 0.9 copy.40
  47.2 0.0 reduce-scatter.9.cloned.1.call-update
  47.2 0.0 reduce-scatter.11.cloned.1.call-start
  47.3 13.6 %reduce-scatter.13.cloned.1.call-done = f32[192,64]{1,0:T(8,128)} async-done(((f32[1536,64]{1,0:T(8,128)}), f32[192,64]{1,0:T(8,128)}) %reduce-scatter.13.cloned.1.call-update) | async-done | bytes 49168
  60.9 1.0 copy.33
  61.8 14.2 %all-gather.1 = bf16[8,192,64]{1,2,0:T(8,128)(2,1)S(1)} all-gather(bf16[1,192,64]{1,2,0:T(8,128)(2,1)S(1)} %bitcast.62), channel_id=1, replica_groups=mesh['user'=4,'item'=8] {'item'}, dimensions={0}, use_global_device_ids=true | all-gather | bytes 221184 | tf_op jit(solution)/shard_map/all_gather | solution.py:47
  76.0 0.1 copy.29
  76.2 0.3 reshape.61
  76.6 0.6 gather_fusion.3
  77.2 0.5 fusion.8
  77.7 0.0 copy-start
  77.7 1.1 fusion
  78.8 0.9 copy.41
  79.7 0.0 reduce-scatter.11.cloned.1.call-update
  79.7 0.0 reduce-scatter.15.cloned.1.call-start
  79.8 7.8 %reduce-scatter.9.cloned.1.call-done = f32[512,64]{0,1:T(8,128)} async-done(((f32[2048,64]{0,1:T(8,128)}), f32[512,64]{0,1:T(8,128)}) %reduce-scatter.9.cloned.1.call-update) | async-done | bytes 131088 | tf_op jit(solution)/shard_map/reduce_scatter | solution.py:55
  87.5 27.6 %reduce-scatter.11.cloned.1.call-done = f32[512,64]{0,1:T(8,128)} async-done(((f32[2048,64]{0,1:T(8,128)}), f32[512,64]{0,1:T(8,128)}) %reduce-scatter.11.cloned.1.call-update) | async-done | bytes 131088 | tf_op jit(solution)/shard_map/reduce_scatter | solution.py:55
  115.2 0.0 copy-done
  115.2 1.6 multiply_convert_fusion.1
  116.8 8.9 %all_gather.14 = bf16[2048,64]{0,1:T(8,128)(2,1)S(1)} all-gather(bf16[512,64]{0,1:T(8,128)(2,1)S(1)} %get-tuple-element.5), channel_id=1, replica_groups=mesh['user'=4,'item'=8] {'user'}, dimensions={0}, use_global_device_ids=true | all-gather | bytes 327680 | tf_op jit(solution)/shard_map/all_gather | solution.py:51
  125.7 0.6 gather_fusion.2
  126.3 0.8 fusion.10
  127.1 1.1 fusion.2
  128.2 1.2 copy.37
  129.4 0.0 reduce-scatter.15.cloned.1.call-update
  129.4 31.6 %reduce-scatter.15.cloned.1.call-done = f32[192,64]{1,0:T(8,128)} async-done(((f32[1536,64]{1,0:T(8,128)}), f32[192,64]{1,0:T(8,128)}) %reduce-scatter.15.cloned.1.call-update) | async-done | bytes 49168
  161.0 1.0 copy.35
  162.0 0.6 multiply_convert_fusion.2
  (11 shorter events, 0.1 us)
Async XLA Ops:
  7.2 15.7 %copy-start.3 = (s32[1,16]{1,0:T(1,128)S(1)}, s32[1,16]{1,0:T(1,128)}, u32[]{:S(2)}) copy-start(s32[1,16]{1,0:T(1,128)} %param.15) | copy-start | bytes 196
  7.2 53.7 %reduce-scatter.13.cloned.1.call-start = ((), (), s32[]{:S(2)}) async-start(), calls=%async_computation.6 | async-start | bytes 884736
  26.4 2.4 %copy-start.1 = (bf16[192,64]{0,1:T(8,128)(2,1)S(1)}, bf16[192,64]{0,1:T(8,128)(2,1)}, u32[]{:S(2)}) copy-start(bf16[192,64]{0,1:T(8,128)(2,1)} %param.12) | copy-start | bytes 73732
  28.7 58.8 %reduce-scatter.9.cloned.1.call-start = ((), (), s32[]{:S(2)}) async-start(), calls=%async_computation.4 | async-start | bytes 655360 | tf_op jit(solution)/shard_map/reduce_scatter | solution.py:55
  44.5 0.7 copy-start.2
  47.2 68.0 %reduce-scatter.11.cloned.1.call-start = ((), (), s32[]{:S(2)}) async-start(), calls=%async_computation.5 | async-start | bytes 655360 | tf_op jit(solution)/shard_map/reduce_scatter | solution.py:55
  77.7 37.5 %copy-start = (bf16[512,64]{0,1:T(8,128)(2,1)S(1)}, bf16[512,64]{0,1:T(8,128)(2,1)}, u32[]{:S(2)}) copy-start(bf16[512,64]{0,1:T(8,128)(2,1)} %param.13) | copy-start | bytes 196612
  79.7 81.3 %reduce-scatter.15.cloned.1.call-start = ((), (), s32[]{:S(2)}) async-start(), calls=%async_computation.7 | async-start | bytes 884736
Sparse Core Ops, SparseCore 0:
  28.8 31.9 reduce-scatter.12
  63.9 23.5 reduce-scatter.8
  90.4 24.7 reduce-scatter.10
  129.5 31.4 reduce-scatter.14
where the time goes:
time: 170 us; the launch traced here: 169 us
  waiting for transfers between devices  80.7 us (47%)
  blocking collectives  48.5 us (29%)
  between operations  14.7 us (9%)
  local copies, waits for them, and re-layouts  9.78 us (6%)
  matrix products  7.78 us (5%)
  other arithmetic  7.61 us (4%)
    unnamed x6, waiting for transfers between devices  45.3 us
    reduce_scatter x2, waiting for transfers between devices, settle_items(): return lax.psum_scatter(terms, 'user', scatter_dimension=0, tiled=True)  35.4 us
    all_gather x2, blocking collectives, spread_users(): return lax.all_gather(piece, 'item', axis=0, tiled=True)  28.8 us
    all_gather x2, blocking collectives, spread_items(): return lax.all_gather(piece, 'user', axis=0, tiled=True)  19.6 us
    unnamed x14, local copies, waits for them, and re-layouts  6.38 us
  transfers between devices with their start and end apart: 4, of which 4 were waited for; matrix products, arithmetic and copies ran while one was open for 5% of the time, Pallas kernels for 0%

commit v1 on v0

v1 whole, which is shorter than its diff:
```python
import functools

import jax
import jax.numpy as jnp
from jax import lax
from jax.experimental import pallas as pl
from jax.experimental.pallas import tpu as pltpu
from jax.sharding import PartitionSpec as P

F32 = jnp.float32
BF16 = jnp.bfloat16
MESH = pl.DeviceIdType.MESH


def kernel(
    sizes, user_cot, item_cot, weight, rows, cols, count, user_deg, item_deg,
    user_grad, item_grad,
    raw, adj, adj_t, row_scale, col_scale, user_panel, item_panel, to_user, to_item,
    user_flat, user_pack, item_pack,
    ag_user, ag_item, out_user, out_item, in_user, in_item,
    load_sem, ag_send_u, ag_recv_u, ag_send_i, ag_recv_i, rs_send_u, rs_recv_u, rs_send_i, rs_recv_i,
):
    n_user, n_item, slots, tile, width, row_tiles, col_tiles = sizes
    me_u, me_i = lax.axis_index("user"), lax.axis_index("item")
    half_u, half_i = user_pack.shape[1], item_pack.shape[1]

    for t in range(slots):
        pltpu.make_async_copy(weight.at[t], raw.at[t], load_sem.at[t]).start()

    barrier = pltpu.get_barrier_semaphore()

    def greet(axis, me, n):
        def step(k, carry):
            pl.semaphore_signal(
                barrier, inc=1, device_id={axis: lax.rem(me + k, n)}, device_id_type=MESH
            )
            return carry
        lax.fori_loop(1, n, step, 0)

    greet("item", me_i, n_item)
    greet("user", me_u, n_user)

    def pack(lo, hi):
        return jnp.concatenate([lo, hi], axis=1)

    own_u = pack(user_cot[0:half_u, :], user_cot[half_u : 2 * half_u, :])
    own_i = pack(item_cot[0:half_i, :], item_cot[half_i : 2 * half_i, :])
    user_pack[0] = own_u
    item_pack[0] = own_i
    ag_user[0, me_i] = own_u
    ag_item[0, me_u] = own_i

    pl.semaphore_wait(barrier, n_user + n_item - 2)

    def gather_copy(axis, me, n, buf, send, recv, hop, k):
        there = lax.rem(me + k, n)
        return pltpu.make_async_remote_copy(
            src_ref=buf.at[hop, me], dst_ref=buf.at[hop, me],
            send_sem=send.at[hop, there], recv_sem=recv.at[hop, me],
            device_id={axis: there}, device_id_type=MESH,
        )

    def gather_wait(axis, me, n, buf, send, recv, hop, k):
        there = lax.rem(me + k, n)
        return pltpu.make_async_remote_copy(
            src_ref=buf.at[hop, me], dst_ref=buf.at[hop, there],
            send_sem=send.at[hop, there], recv_sem=recv.at[hop, there],
            device_id={axis: there}, device_id_type=MESH,
        )

    def settle_copy(axis, me, n, src, dst, send, recv, hop, k):
        there = lax.rem(me + k, n)
        return pltpu.make_async_remote_copy(
            src_ref=src.at[hop, there], dst_ref=dst.at[hop, me],
            send_sem=send.at[hop, there], recv_sem=recv.at[hop, me],
            device_id={axis: there}, device_id_type=MESH,
        )

    def settle_wait(axis, me, n, src, dst, send, recv, hop, k):
        there = lax.rem(me + k, n)
        return pltpu.make_async_remote_copy(
            src_ref=src.at[hop, there], dst_ref=dst.at[hop, there],
            send_sem=send.at[hop, there], recv_sem=recv.at[hop, there],
            device_id={axis: there}, device_id_type=MESH,
        )

    AG_U = ("item", me_i, n_item, ag_user, ag_send_u, ag_recv_u)
    AG_I = ("user", me_u, n_user, ag_item, ag_send_i, ag_recv_i)
    RS_U = ("item", me_i, n_item, out_user, in_user, rs_send_u, rs_recv_u)
    RS_I = ("user", me_u, n_user, out_item, in_item, rs_send_i, rs_recv_i)

    def each(n, fn):
        def step(k, carry):
            fn(k)
            return carry
        lax.fori_loop(1, n, step, 0)

    def start_gather(g, hop):
        each(g[2], lambda k: gather_copy(*g, hop, k).start())

    def end_gather(g, hop):
        each(g[2], lambda k: gather_wait(*g, hop, k).wait_recv())

    def start_settle(s, hop):
        each(s[2], lambda k: settle_copy(*s, hop, k).start())

    def end_settle(s, hop):
        each(s[2], lambda k: settle_wait(*s, hop, k).wait_recv())

    start_gather(AG_U, 0)
    start_gather(AG_I, 0)

    for r in range(row_tiles):
        scale = lax.rsqrt(user_deg[:, r * tile : (r + 1) * tile].astype(F32))
        row_scale[r] = jnp.transpose(jnp.broadcast_to(scale, (128, tile)))
    for c in range(col_tiles):
        col_scale[c] = lax.rsqrt(item_deg[:, c * tile : (c + 1) * tile].astype(F32))
    row_id = [rows[0, t] for t in range(slots)]
    col_id = [cols[0, t] for t in range(slots)]

    def chain(ids, blocks):
        before = []
        for t in range(slots):
            prev = jnp.int32(slots)
            for s in range(t):
                prev = jnp.where(ids[s] == ids[t], jnp.int32(s), prev)
            before.append(prev)
        last = []
        for b in range(blocks):
            found = jnp.int32(slots)
            for t in range(slots):
                found = jnp.where(ids[t] == b, jnp.int32(t), found)
            last.append(found)
        return before, last

    row_before, row_last = chain(row_id, row_tiles)
    col_before, col_last = chain(col_id, col_tiles)
    to_user[slots] = jnp.zeros((tile, width), F32)
    to_item[slots] = jnp.zeros((tile, width), F32)
    live = count[0, 0]
    for t in range(slots):
        pltpu.make_async_copy(weight.at[t], raw.at[t], load_sem.at[t]).wait()
        on = jnp.where(t < live, jnp.float32(1), jnp.float32(0))
        rs = row_scale[row_id[t]]
        cs = col_scale[col_id[t]] * on
        w = raw[t].astype(F32)
        a = jnp.concatenate(
            [(w[:, j : j + 128] * rs) * cs[:, j : j + 128] for j in range(0, tile, 128)], axis=1
        ).astype(BF16)
        adj[t] = a
        adj_t[t] = jnp.transpose(a)

    def unpack(buf, hop, n, half, panel):
        for p in range(n):
            block = buf[hop, p]
            for side in range(2):
                part = block[:, side * width : (side + 1) * width]
                at, done = (2 * p + side) * half, 0
                while done < half:
                    b, off = divmod(at + done, tile)
                    size = min(half - done, tile - off)
                    panel[b, off : off + size, :] = part[done : done + size, :]
                    done += size

    def user_terms(hop):
        end_gather(AG_I, hop)
        unpack(ag_item, hop, n_user, half_i, item_panel)
        for t in range(slots):
            to_user[t] = to_user[row_before[t]] + jnp.dot(
                adj[t], item_panel[col_id[t]], preferred_element_type=F32
            )
        for r in range(row_tiles):
            user_flat[r * tile : (r + 1) * tile, :] = to_user[row_last[r]]
        for p in range(n_item):
            at = 2 * p * half_u
            out_user[hop, p] = pack(
                user_flat[at : at + half_u, :], user_flat[at + half_u : at + 2 * half_u, :]
            ).astype(out_user.dtype)
        in_user[hop, me_i] = out_user[hop, me_i]
        start_settle(RS_U, hop)

    def item_terms(hop):
        end_gather(AG_U, hop)
        unpack(ag_user, hop, n_item, half_u, user_panel)
        for t in range(slots):
            to_item[t] = to_item[col_before[t]] + jnp.dot(
                adj_t[t], user_panel[row_id[t]], preferred_element_type=F32
            )
        whole = [to_item[col_last[c]] for c in range(col_tiles)]

        def piece(at):
            b, off = divmod(at, tile)
            return whole[b][off : off + half_i, :]

        for p in range(n_user):
            out_item[hop, p] = pack(
                piece(2 * p * half_i), piece((2 * p + 1) * half_i)
            ).astype(out_item.dtype)
        in_item[hop, me_u] = out_item[hop, me_u]
        start_settle(RS_I, hop)

    def total(s, hop):
        end_settle(s, hop)
        dst = s[4]
        acc = dst[hop, 0].astype(F32)
        for p in range(1, s[2]):
            acc = acc + dst[hop, p].astype(F32)
        return acc

    user_terms(0)
    item_terms(0)
    once_i = total(RS_I, 0).astype(BF16)
    ag_item[1, me_u] = once_i
    start_gather(AG_I, 1)
    item_pack[1] = once_i
    once_u = total(RS_U, 0).astype(BF16)
    ag_user[1, me_i] = once_u
    start_gather(AG_U, 1)
    user_pack[1] = once_u
    user_terms(1)
    item_terms(1)

    def finish(s, packed, out, half):
        twice = total(s, 1)
        grad = ((packed[0].astype(F32) + packed[1].astype(F32) + twice) / 3.0).astype(BF16)
        out[0:half, :] = grad[:, 0:width]
        out[half : 2 * half, :] = grad[:, width : 2 * width]

    finish(RS_I, item_pack, item_grad, half_i)
    finish(RS_U, user_pack, user_grad, half_u)

    for hop in range(2):
        each(n_item, lambda k: gather_copy(*AG_U, hop, k).wait_send())
        each(n_user, lambda k: gather_copy(*AG_I, hop, k).wait_send())
        each(n_item, lambda k: settle_copy(*RS_U, hop, k).wait_send())
        each(n_user, lambda k: settle_copy(*RS_I, hop, k).wait_send())


def shards(n_user, n_item, user_cot, item_cot, tile_weight, tile_rows, tile_cols, tile_count, user_degree, item_degree):
    slots, tile = tile_weight.shape[0], tile_weight.shape[2]
    width = user_cot.shape[1]
    shard_users, shard_items = user_degree.shape[0], item_degree.shape[0]
    row_tiles, col_tiles = shard_users // tile, shard_items // tile
    half_u, half_i = user_cot.shape[0] // 2, item_cot.shape[0] // 2
    sizes = (n_user, n_item, slots, tile, width, row_tiles, col_tiles)
    sent = BF16
    vmem = pl.BlockSpec(memory_space=pltpu.VMEM)
    smem = pl.BlockSpec(memory_space=pltpu.SMEM)
    dma = pltpu.SemaphoreType.DMA
    return pl.pallas_call(
        functools.partial(kernel, sizes),
        out_shape=(
            jax.ShapeDtypeStruct(user_cot.shape, BF16),
            jax.ShapeDtypeStruct(item_cot.shape, BF16),
        ),
        in_specs=[vmem, vmem, pl.BlockSpec(memory_space=pl.ANY), smem, smem, smem, vmem, vmem],
        out_specs=(vmem, vmem),
        scratch_shapes=[
            pltpu.VMEM((slots, tile, tile), jnp.int32),
            pltpu.VMEM((slots, tile, tile), BF16),
            pltpu.VMEM((slots, tile, tile), BF16),
            pltpu.VMEM((row_tiles, tile, 128), F32),
            pltpu.VMEM((col_tiles, 1, tile), F32),
            pltpu.VMEM((row_tiles, tile, width), BF16),
            pltpu.VMEM((col_tiles, tile, width), BF16),
            pltpu.VMEM((slots + 1, tile, width), F32),
            pltpu.VMEM((slots + 1, tile, width), F32),
            pltpu.VMEM((shard_users, width), F32),
            pltpu.VMEM((2, half_u, 2 * width), BF16),
            pltpu.VMEM((2, half_i, 2 * width), BF16),
            pltpu.VMEM((2, n_item, half_u, 2 * width), BF16),
            pltpu.VMEM((2, n_user, half_i, 2 * width), BF16),
            pltpu.VMEM((2, n_item, half_u, 2 * width), sent),
            pltpu.VMEM((2, n_user, half_i, 2 * width), sent),
            pltpu.VMEM((2, n_item, half_u, 2 * width), sent),
            pltpu.VMEM((2, n_user, half_i, 2 * width), sent),
            dma((slots,)),
            dma((2, n_item)), dma((2, n_item)), dma((2, n_user)), dma((2, n_user)),
            dma((2, n_item)), dma((2, n_item)), dma((2, n_user)), dma((2, n_user)),
        ],
        compiler_params=pltpu.CompilerParams(
            collective_id=0, has_side_effects=True, vmem_limit_bytes=40 * 1024 * 1024
        ),
    )(
        user_cot, item_cot, tile_weight, tile_rows, tile_cols, tile_count,
        user_degree.reshape(1, shard_users), item_degree.reshape(1, shard_items),
    )


def solution(mesh):
    return jax.shard_map(
        functools.partial(shards, mesh.shape["user"], mesh.shape["item"]),
        mesh=mesh,
        in_specs=(
            P(("user", "item"), None),
            P(("item", "user"), None),
            P("user", "item", None),
            P("user", "item"),
            P("user", "item"),
            P("user", "item"),
            P("user"),
            P("item"),
        ),
        out_specs=(P(("user", "item"), None), P(("item", "user"), None)),
        check_vma=False,
    )
```

time: 170 us -> 41.6 us (0.24)
  waiting for transfers between devices: 80.7 us -> 0 us
  blocking collectives: 48.5 us -> 0 us
  Pallas kernels: 0 us -> 31.7 us
  between operations: 14.7 us -> 1.31 us
  matrix products: 7.78 us -> 0 us
  other arithmetic: 7.61 us -> 0 us
    all_gather x4 -> x0, blocking collectives: 48.5 us -> none  [the longest x2 28.8 us: spread_users(): return lax.all_gather(piece, 'item', axis=0, tiled=True)]
    unnamed x6 -> x0, waiting for transfers between devices: 45.3 us -> none
    reduce_scatter x2 -> x0, waiting for transfers between devices: 35.4 us -> none  [settle_items(): return lax.psum_scatter(terms, 'user', scatter_dimension=0, tiled=True)]
    pallas_call x0 -> x1, Pallas kernels: none -> 31.7 us  [shards(): pl.pallas_call(functools.partial(kernel, sizes), out_shape=(jax.ShapeDtyp...]
    dot_general x10 -> x0, matrix products: 7.78 us -> none  [the longest x2 2.11 us: toward_users(): jnp.einsum('tb,trd->brd', row_onehot, contrib, precision=lax.Precision.HI...]
    convert_element_type x4 -> x0, other arithmetic: 4.86 us -> none  [the longest x1 2.6 us: build_tiles(): adjacency = (weights.astype(jnp.float32) * row_factor[:, :, None] * col_f...]
    gather x4 -> x0, local copies, waits for them, and re-layouts: 2.33 us -> none  [the longest x2 1.17 us: toward_users(): blocks = jnp.take(panel, col_ids, axis=0)]
    unnamed x14 -> x10, local copies, waits for them, and re-layouts: 6.38 us -> 6.02 us
  transfers between devices with their start and end apart: 4 -> 0, of which waited for: 4 -> 0; matrix products, arithmetic and copies ran while one was open for 5% -> 0% of each run, Pallas kernels for 0% -> 0%
where the time goes in v1:
time: 41.6 us; the launch traced here: 41.2 us
  Pallas kernels  31.7 us (76%)
  local copies, waits for them, and re-layouts  8.16 us (20%)
  between operations  1.31 us (3%)
    pallas_call x1, Pallas kernels, shards(): pl.pallas_call(functools.partial(kernel, sizes), out_shape=(jax.ShapeDtyp...  31.7 us
    unnamed x10, local copies, waits for them, and re-layouts  6.02 us
    pallas_call x2, local copies, waits for them, and re-layouts, shards(): pl.pallas_call(functools.partial(kernel, sizes), out_shape=(jax.ShapeDtyp...  1.44 us

profile of v1, /device:TPU:0, one launch (start us, length us, event | category | flops | bytes accessed | tf_op | source)
XLA Modules:
  0.0 41.2 jit_solution(11343575262411087408)
XLA Ops:
  1.3 0.7 %reshape.10.user_deg = s32[1,1536]{1,0:T(1,128)S(1)} reshape(s32[1536]{0:T(1024)} %param.14) | data formatting | bytes 12288 | tf_op jit(solution)/shard_map/reshape | solution.py:286
  2.0 0.9 %copy.10.user_cot = bf16[192,64]{1,0:T(8,128)(2,1)S(1)} copy(bf16[192,64]{0,1:T(8,128)(2,1)} %param.8) | data formatting | bytes 49152 | tf_op args[0]
  2.8 1.0 %copy.11.item_cot = bf16[512,64]{1,0:T(8,128)(2,1)S(1)} copy(bf16[512,64]{0,1:T(8,128)(2,1)} %param.9) | data formatting | bytes 131072 | tf_op args[1]
  3.8 0.0 copy-start
  3.8 2.2 %copy-done = s32[16,256,256]{2,1,0:T(8,128)S(1)} copy-done((s32[16,256,256]{2,1,0:T(8,128)S(1)}, s32[16,256,256]{2,1,0:T(8,128)}, u32[]{:S(2)}) %copy-start) | copy-done | bytes 4194328
  6.0 0.0 copy-start.1
  6.0 0.7 %copy-done.1 = s32[2048]{0:T(1024)S(1)} copy-done((s32[2048]{0:T(1024)S(1)}, s32[2048]{0:T(1024)}, u32[]{:S(2)}) %copy-start.1) | copy-done | bytes 8216
  6.7 0.0 copy-start.2
  6.7 0.7 %copy-done.2 = s32[1,16]{1,0:T(1,128)S(1)} copy-done((s32[1,16]{1,0:T(1,128)S(1)}, s32[1,16]{1,0:T(1,128)}, u32[]{:S(2)}) %copy-start.2) | copy-done | bytes 88
  7.4 0.0 copy-start.3
  7.4 0.7 %copy-done.3 = s32[1,16]{1,0:T(1,128)S(1)} copy-done((s32[1,16]{1,0:T(1,128)S(1)}, s32[1,16]{1,0:T(1,128)}, u32[]{:S(2)}) %copy-start.3) | copy-done | bytes 88
  8.0 31.7 %shard_map.95 = (bf16[192,64]{1,0:T(8,128)(2,1)S(1)}, bf16[512,64]{1,0:T(8,128)(2,1)S(1)}) custom-call(bf16[192,64]{1,0:T(8,128)(2,1)S(1)} %copy.10.user_cot, bf16[512,64]{1,0:T(8,128)(2,1)S(1)} %copy.11.item_cot, s32[16,256,256]{2,1,0:T(8,128)S(1)} %copy-done, s32[1,16]{1,0:T(1,128)S(1)} %copy-done.2, s32[1,16]{1,0:T(1,128)S(1)} %copy-done.3, ...), custom_call_target="tpu_custom_call" | custom-call | tf_op jit(solution)/shard_map/pallas_call | solution.py:250
  39.8 0.7 %copy.12 = bf16[192,64]{0,1:T(8,128)(2,1)} copy(bf16[192,64]{1,0:T(8,128)(2,1)S(1)} %get-tuple-element.2) | data formatting | bytes 49152 | tf_op jit(solution)/shard_map/pallas_call | solution.py:250
  40.5 0.7 %copy.13 = bf16[512,64]{0,1:T(8,128)(2,1)} copy(bf16[512,64]{1,0:T(8,128)(2,1)S(1)} %get-tuple-element.3) | data formatting | bytes 131072 | tf_op jit(solution)/shard_map/pallas_call | solution.py:250
Async XLA Ops:
  3.8 2.2 %copy-start = (s32[16,256,256]{2,1,0:T(8,128)S(1)}, s32[16,256,256]{2,1,0:T(8,128)}, u32[]{:S(2)}) copy-start(s32[16,256,256]{2,1,0:T(8,128)} %weight.1) | copy-start | bytes 12582916
  6.0 0.7 %copy-start.1 = (s32[2048]{0:T(1024)S(1)}, s32[2048]{0:T(1024)}, u32[]{:S(2)}) copy-start(s32[2048]{0:T(1024)} %param.15) | copy-start | bytes 24580
  6.7 0.7 %copy-start.2 = (s32[1,16]{1,0:T(1,128)S(1)}, s32[1,16]{1,0:T(1,128)}, u32[]{:S(2)}) copy-start(s32[1,16]{1,0:T(1,128)} %rows.1) | copy-start | bytes 196
  7.4 0.7 %copy-start.3 = (s32[1,16]{1,0:T(1,128)S(1)}, s32[1,16]{1,0:T(1,128)}, u32[]{:S(2)}) copy-start(s32[1,16]{1,0:T(1,128)} %cols.1) | copy-start | bytes 196

commit v2 on v1

--- a/solution.py
+++ b/solution.py
@@ -1,4 +1,5 @@
 import functools
+import math
 
 import jax
 import jax.numpy as jnp
@@ -13,17 +14,27 @@
 
 
 def kernel(
-    sizes, user_cot, item_cot, weight, rows, cols, count, user_deg, item_deg,
+    sizes, user_cot, item_cot, weight, rows_in, cols_in, count_in, user_deg, item_deg,
     user_grad, item_grad,
-    raw, adj, adj_t, row_scale, col_scale, user_panel, item_panel, to_user, to_item,
-    user_flat, user_pack, item_pack,
+    cot_u, cot_i, deg_u, deg_i, rows, cols, count,
+    raw, adj, row_scale, col_scale, user_panel, item_panel, to_user, to_item,
+    user_pack, item_pack,
     ag_user, ag_item, out_user, out_item, in_user, in_item,
-    load_sem, ag_send_u, ag_recv_u, ag_send_i, ag_recv_i, rs_send_u, rs_recv_u, rs_send_i, rs_recv_i,
+    load_sem, small_sem, ag_send_u, ag_recv_u, ag_send_i, ag_recv_i, rs_send_u, rs_recv_u, rs_send_i, rs_recv_i,
 ):
     n_user, n_item, slots, tile, width, row_tiles, col_tiles = sizes
     me_u, me_i = lax.axis_index("user"), lax.axis_index("item")
-    half_u, half_i = user_pack.shape[1], item_pack.shape[1]
-
+    piece_u, piece_i = cot_u.shape[1], cot_i.shape[1]
+
+    small = [
+        pltpu.make_async_copy(src, dst, small_sem.at[j])
+        for j, (src, dst) in enumerate([
+            (user_cot, cot_u), (item_cot, cot_i), (user_deg, deg_u), (item_deg, deg_i),
+            (rows_in, rows), (cols_in, cols), (count_in, count),
+        ])
+    ]
+    for copy in small:
+        copy.start()
     for t in range(slots):
         pltpu.make_async_copy(weight.at[t], raw.at[t], load_sem.at[t]).start()
 
@@ -40,15 +51,37 @@
     greet("item", me_i, n_item)
     greet("user", me_u, n_user)
 
-    def pack(lo, hi):
-        return jnp.concatenate([lo, hi], axis=1)
-
-    own_u = pack(user_cot[0:half_u, :], user_cot[half_u : 2 * half_u, :])
-    own_i = pack(item_cot[0:half_i, :], item_cot[half_i : 2 * half_i, :])
-    user_pack[0] = own_u
-    item_pack[0] = own_i
-    ag_user[0, me_i] = own_u
-    ag_item[0, me_u] = own_i
+    grain = math.gcd(piece_u, 128)
+    folds, whole_lanes = 128 // grain, piece_u // 128 * 128
+    fold_rows, main_rows = width // folds, width * (piece_u // 128)
+
+    def fold_in(put, take):
+        for j in range(0, whole_lanes, 128):
+            put(j // 128 * width, take(j, 128))
+        if whole_lanes < piece_u:
+            rest = take(whole_lanes, grain)
+            put(main_rows, jnp.concatenate(
+                [rest[f * fold_rows : (f + 1) * fold_rows, :] for f in range(folds)], axis=1))
+
+    def unfold(wire, lane, size):
+        if lane < whole_lanes:
+            at = lane // 128 * width
+            return wire[at : at + width, lane % 128 : lane % 128 + size]
+        rest = wire[main_rows : main_rows + fold_rows, :]
+        return jnp.concatenate(
+            [rest[:, f * grain : (f + 1) * grain] for f in range(folds)], axis=0)
+
+    for copy in small[:2]:
+        copy.wait()
+    own = cot_u[...]
+
+    def put_own(at, value):
+        user_pack[0, at : at + value.shape[0], :] = value
+
+    fold_in(put_own, lambda lane, size: own[:, lane : lane + size])
+    item_pack[0] = cot_i[...]
+    ag_user[0, me_i] = user_pack[0]
+    ag_item[0, me_u] = item_pack[0]
 
     pl.semaphore_wait(barrier, n_user + n_item - 2)
 
@@ -110,11 +143,13 @@
     start_gather(AG_U, 0)
     start_gather(AG_I, 0)
 
+    for copy in small[2:]:
+        copy.wait()
     for r in range(row_tiles):
-        scale = lax.rsqrt(user_deg[:, r * tile : (r + 1) * tile].astype(F32))
+        scale = lax.rsqrt(deg_u[r * tile : (r + 1) * tile].astype(F32)).reshape(1, tile)
         row_scale[r] = jnp.transpose(jnp.broadcast_to(scale, (128, tile)))
     for c in range(col_tiles):
-        col_scale[c] = lax.rsqrt(item_deg[:, c * tile : (c + 1) * tile].astype(F32))
+        col_scale[c] = lax.rsqrt(deg_i[c * tile : (c + 1) * tile].astype(F32)).reshape(1, tile)
     row_id = [rows[0, t] for t in range(slots)]
     col_id = [cols[0, t] for t in range(slots)]
 
@@ -135,8 +170,8 @@
 
     row_before, row_last = chain(row_id, row_tiles)
     col_before, col_last = chain(col_id, col_tiles)
-    to_user[slots] = jnp.zeros((tile, width), F32)
-    to_item[slots] = jnp.zeros((tile, width), F32)
+    to_user[slots] = jnp.zeros((width, tile), F32)
+    to_item[slots] = jnp.zeros((width, tile), F32)
     live = count[0, 0]
     for t in range(slots):
         pltpu.make_async_copy(weight.at[t], raw.at[t], load_sem.at[t]).wait()
@@ -148,54 +183,61 @@
             [(w[:, j : j + 128] * rs) * cs[:, j : j + 128] for j in range(0, tile, 128)], axis=1
         ).astype(BF16)
         adj[t] = a
-        adj_t[t] = jnp.transpose(a)
-
-    def unpack(buf, hop, n, half, panel):
-        for p in range(n):
-            block = buf[hop, p]
-            for side in range(2):
-                part = block[:, side * width : (side + 1) * width]
-                at, done = (2 * p + side) * half, 0
-                while done < half:
-                    b, off = divmod(at + done, tile)
-                    size = min(half - done, tile - off)
-                    panel[b, off : off + size, :] = part[done : done + size, :]
-                    done += size
 
     def user_terms(hop):
         end_gather(AG_I, hop)
-        unpack(ag_item, hop, n_user, half_i, item_panel)
+        for p in range(n_user):
+            for lane in range(0, piece_i, 128):
+                b, off = divmod(p * piece_i + lane, tile)
+                item_panel[b, :, off : off + 128] = ag_item[hop, p, :, lane : lane + 128]
         for t in range(slots):
-            to_user[t] = to_user[row_before[t]] + jnp.dot(
-                adj[t], item_panel[col_id[t]], preferred_element_type=F32
+            to_user[t] = to_user[row_before[t]] + lax.dot_general(
+                item_panel[col_id[t]], adj[t], (((1,), (1,)), ((), ())),
+                preferred_element_type=F32,
             )
-        for r in range(row_tiles):
-            user_flat[r * tile : (r + 1) * tile, :] = to_user[row_last[r]]
+        tiles = [to_user[row_last[r]].astype(out_user.dtype) for r in range(row_tiles)]
+
+        def lanes(at, size):
+            parts = []
+            while size:
+                b, off = divmod(at, tile)
+                step = size if off % 128 == 0 and off + size <= tile else grain
+                parts.append(tiles[b][:, off : off + step])
+                at, size = at + step, size - step
+            return parts[0] if len(parts) == 1 else jnp.concatenate(parts, axis=1)
+
         for p in range(n_item):
-            at = 2 * p * half_u
-            out_user[hop, p] = pack(
-                user_flat[at : at + half_u, :], user_flat[at + half_u : at + 2 * half_u, :]
-            ).astype(out_user.dtype)
+            def put(at, value):
+                out_user[hop, p, at : at + value.shape[0], :] = value
+
+            fold_in(put, lambda lane, size: lanes(p * piece_u + lane, size))
         in_user[hop, me_i] = out_user[hop, me_i]
         start_settle(RS_U, hop)
 
     def item_terms(hop):
         end_gather(AG_U, hop)
-        unpack(ag_user, hop, n_item, half_u, user_panel)
+        wires = [ag_user[hop, p] for p in range(n_item)]
+        for at in range(0, n_item * piece_u, 128):
+            p, lane = divmod(at, piece_u)
+            if lane % 128 == 0 and lane < whole_lanes:
+                block = unfold(wires[p], lane, 128)
+            else:
+                parts = []
+                for g in range(at, at + 128, grain):
+                    p, lane = divmod(g, piece_u)
+                    parts.append(unfold(wires[p], lane, grain))
+                block = jnp.concatenate(parts, axis=1)
+            b, off = divmod(at, tile)
+            user_panel[b, :, off : off + 128] = block
         for t in range(slots):
             to_item[t] = to_item[col_before[t]] + jnp.dot(
-                adj_t[t], user_panel[row_id[t]], preferred_element_type=F32
+                user_panel[row_id[t]], adj[t], preferred_element_type=F32
             )
-        whole = [to_item[col_last[c]] for c in range(col_tiles)]
-
-        def piece(at):
-            b, off = divmod(at, tile)
-            return whole[b][off : off + half_i, :]
-
-        for p in range(n_user):
-            out_item[hop, p] = pack(
-                piece(2 * p * half_i), piece((2 * p + 1) * half_i)
-            ).astype(out_item.dtype)
+        for c in range(col_tiles):
+            done = to_item[col_last[c]].astype(out_item.dtype)
+            for lane in range(0, tile, 128):
+                p, off = divmod(c * tile + lane, piece_i)
+                out_item[hop, p, :, off : off + 128] = done[:, lane : lane + 128]
         in_item[hop, me_u] = out_item[hop, me_u]
         start_settle(RS_I, hop)
 
@@ -220,14 +262,16 @@
     user_terms(1)
     item_terms(1)
 
-    def finish(s, packed, out, half):
+    def finish(s, packed):
         twice = total(s, 1)
-        grad = ((packed[0].astype(F32) + packed[1].astype(F32) + twice) / 3.0).astype(BF16)
-        out[0:half, :] = grad[:, 0:width]
-        out[half : 2 * half, :] = grad[:, width : 2 * width]
-
-    finish(RS_I, item_pack, item_grad, half_i)
-    finish(RS_U, user_pack, user_grad, half_u)
+        return ((packed[0].astype(F32) + packed[1].astype(F32) + twice) / 3.0).astype(BF16)
+
+    item_grad[...] = finish(RS_I, item_pack)
+    wire = finish(RS_U, user_pack)
+    for lane in range(0, whole_lanes, 128):
+        user_grad[:, lane : lane + 128] = unfold(wire, lane, 128)
+    if whole_lanes < piece_u:
+        user_grad[:, whole_lanes:piece_u] = unfold(wire, whole_lanes, grain)
 
     for hop in range(2):
         each(n_item, lambda k: gather_copy(*AG_U, hop, k).wait_send())
@@ -241,50 +285,57 @@
     width = user_cot.shape[1]
     shard_users, shard_items = user_degree.shape[0], item_degree.shape[0]
     row_tiles, col_tiles = shard_users // tile, shard_items // tile
-    half_u, half_i = user_cot.shape[0] // 2, item_cot.shape[0] // 2
+    piece_u, piece_i = user_cot.shape[0], item_cot.shape[0]
+    wire_u = (width * piece_u // 128, 128)
+    wire_i = (width, piece_i)
     sizes = (n_user, n_item, slots, tile, width, row_tiles, col_tiles)
     sent = BF16
     vmem = pl.BlockSpec(memory_space=pltpu.VMEM)
-    smem = pl.BlockSpec(memory_space=pltpu.SMEM)
     dma = pltpu.SemaphoreType.DMA
-    return pl.pallas_call(
+    user_grad, item_grad = pl.pallas_call(
         functools.partial(kernel, sizes),
         out_shape=(
-            jax.ShapeDtypeStruct(user_cot.shape, BF16),
-            jax.ShapeDtypeStruct(item_cot.shape, BF16),
+            jax.ShapeDtypeStruct((width, piece_u), BF16),
+            jax.ShapeDtypeStruct((width, piece_i), BF16),
         ),
-        in_specs=[vmem, vmem, pl.BlockSpec(memory_space=pl.ANY), smem, smem, smem, vmem, vmem],
+        in_specs=[pl.BlockSpec(memory_space=pl.ANY)] * 8,
         out_specs=(vmem, vmem),
         scratch_shapes=[
+            pltpu.VMEM((width, piece_u), BF16),
+            pltpu.VMEM((width, piece_i), BF16),
+            pltpu.VMEM((shard_users,), jnp.int32),
+            pltpu.VMEM((shard_items,), jnp.int32),
+            pltpu.SMEM(tile_rows.shape, jnp.int32),
+            pltpu.SMEM(tile_cols.shape, jnp.int32),
+            pltpu.SMEM(tile_count.shape, jnp.int32),
             pltpu.VMEM((slots, tile, tile), jnp.int32),
-            pltpu.VMEM((slots, tile, tile), BF16),
             pltpu.VMEM((slots, tile, tile), BF16),
             pltpu.VMEM((row_tiles, tile, 128), F32),
             pltpu.VMEM((col_tiles, 1, tile), F32),
-            pltpu.VMEM((row_tiles, tile, width), BF16),
-            pltpu.VMEM((col_tiles, tile, width), BF16),
-            pltpu.VMEM((slots + 1, tile, width), F32),
-            pltpu.VMEM((slots + 1, tile, width), F32),
-            pltpu.VMEM((shard_users, width), F32),
-            pltpu.VMEM((2, half_u, 2 * width), BF16),
-            pltpu.VMEM((2, half_i, 2 * width), BF16),
-            pltpu.VMEM((2, n_item, half_u, 2 * width), BF16),
-            pltpu.VMEM((2, n_user, half_i, 2 * width), BF16),
-            pltpu.VMEM((2, n_item, half_u, 2 * width), sent),
-            pltpu.VMEM((2, n_user, half_i, 2 * width), sent),
-            pltpu.VMEM((2, n_item, half_u, 2 * width), sent),
-            pltpu.VMEM((2, n_user, half_i, 2 * width), sent),
-            dma((slots,)),
+            pltpu.VMEM((row_tiles, width, tile), BF16),
+            pltpu.VMEM((col_tiles, width, tile), BF16),
+            pltpu.VMEM((slots + 1, width, tile), F32),
+            pltpu.VMEM((slots + 1, width, tile), F32),
+            pltpu.VMEM((2, *wire_u), BF16),
+            pltpu.VMEM((2, *wire_i), BF16),
+            pltpu.VMEM((2, n_item, *wire_u), BF16),
+            pltpu.VMEM((2, n_user, *wire_i), BF16),
+            pltpu.VMEM((2, n_item, *wire_u), sent),
+            pltpu.VMEM((2, n_user, *wire_i), sent),
+            pltpu.VMEM((2, n_item, *wire_u), sent),
+            pltpu.VMEM((2, n_user, *wire_i), sent),
+            dma((slots,)), dma((7,)),
             dma((2, n_item)), dma((2, n_item)), dma((2, n_user)), dma((2, n_user)),
             dma((2, n_item)), dma((2, n_item)), dma((2, n_user)), dma((2, n_user)),
         ],
         compiler_params=pltpu.CompilerParams(
-            collective_id=0, has_side_effects=True, vmem_limit_bytes=40 * 1024 * 1024
+            collective_id=0, has_side_effects=True, vmem_limit_bytes=62 * 1024 * 1024
         ),
     )(
-        user_cot, item_cot, tile_weight, tile_rows, tile_cols, tile_count,
-        user_degree.reshape(1, shard_users), item_degree.reshape(1, shard_items),
+        user_cot.T, item_cot.T, tile_weight, tile_rows, tile_cols, tile_count,
+        user_degree, item_degree,
     )
+    return user_grad.T, item_grad.T
 
 
 def solution(mesh):

time: 41.6 us -> 34.6 us (0.83)
  local copies, waits for them, and re-layouts: 8.16 us -> 2.85 us
  Pallas kernels: 31.7 us -> 30.2 us
    unnamed x10 -> x2, local copies, waits for them, and re-layouts: 6.02 us -> 2.85 us
    pallas_call x1, Pallas kernels: 31.7 us -> 30.2 us  [shards(): pl.pallas_call(functools.partial(kernel, sizes), out_shape=(jax.ShapeDtyp...]
    pallas_call x2 -> x0, local copies, waits for them, and re-layouts: 1.44 us -> none  [shards(): pl.pallas_call(functools.partial(kernel, sizes), out_shape=(jax.ShapeDtyp...]
    reshape x1 -> x0, local copies, waits for them, and re-layouts: 0.7 us -> none  [shards(): user_degree.reshape(1, shard_users)]
where the time goes in v2:
time: 34.6 us; the launch traced here: 34.3 us
  Pallas kernels  30.2 us (87%)
  local copies, waits for them, and re-layouts  2.85 us (8%)
  between operations  1.29 us (4%)
    pallas_call x1, Pallas kernels, shards(): pl.pallas_call(functools.partial(kernel, sizes), out_shape=(jax.ShapeDtyp...  30.2 us
    unnamed x2, local copies, waits for them, and re-layouts  2.85 us

profile of v2, /device:TPU:0, one launch (start us, length us, event | category | flops | bytes accessed | tf_op | source)
XLA Modules:
  0.0 34.3 jit_solution(1133075792063292578)
XLA Ops:
  1.3 30.2 %shard_map.95 = (bf16[64,192]{1,0:T(8,128)(2,1)}, bf16[64,512]{1,0:T(8,128)(2,1)}) custom-call(bf16[64,192]{1,0:T(8,128)(2,1)} %bitcast.6, bf16[64,512]{1,0:T(8,128)(2,1)} %bitcast.4, s32[16,256,256]{2,1,0:T(8,128)} %weight.1, s32[1,16]{1,0:T(1,128)} %rows_in.1, s32[1,16]{1,0:T(1,128)} %cols_in.1, s32[1,1]{1,0:T(1,128)S(6)} %copy.12.count_in, ...), custom_call_target="tpu_custom_call" | custom-call | tf_op jit(solution)/shard_map/pallas_call | solution.py:295
  31.5 1.4 %copy.13 = bf16[192,64]{0,1:T(8,128)(2,1)} copy(bf16[192,64]{0,1:T(8,128)(2,1)} %bitcast.7) | data formatting | bytes 49152
  32.8 1.5 %copy.14 = bf16[512,64]{0,1:T(8,128)(2,1)} copy(bf16[512,64]{0,1:T(8,128)(2,1)} %bitcast.5) | data formatting | bytes 131072

commit v3 on v2

--- a/solution.py
+++ b/solution.py
@@ -46,7 +46,11 @@
                 barrier, inc=1, device_id={axis: lax.rem(me + k, n)}, device_id_type=MESH
             )
             return carry
-        lax.fori_loop(1, n, step, 0)
+        if n > 8:
+            lax.fori_loop(1, n, step, 0)
+        else:
+            for k in range(1, n):
+                step(k, 0)
 
     greet("item", me_i, n_item)
     greet("user", me_u, n_user)
@@ -89,15 +93,7 @@
         there = lax.rem(me + k, n)
         return pltpu.make_async_remote_copy(
             src_ref=buf.at[hop, me], dst_ref=buf.at[hop, me],
-            send_sem=send.at[hop, there], recv_sem=recv.at[hop, me],
-            device_id={axis: there}, device_id_type=MESH,
-        )
-
-    def gather_wait(axis, me, n, buf, send, recv, hop, k):
-        there = lax.rem(me + k, n)
-        return pltpu.make_async_remote_copy(
-            src_ref=buf.at[hop, me], dst_ref=buf.at[hop, there],
-            send_sem=send.at[hop, there], recv_sem=recv.at[hop, there],
+            send_sem=send.at[hop], recv_sem=recv.at[hop],
             device_id={axis: there}, device_id_type=MESH,
         )
 
@@ -105,16 +101,15 @@
         there = lax.rem(me + k, n)
         return pltpu.make_async_remote_copy(
             src_ref=src.at[hop, there], dst_ref=dst.at[hop, me],
-            send_sem=send.at[hop, there], recv_sem=recv.at[hop, me],
+            send_sem=send.at[hop], recv_sem=recv.at[hop],
             device_id={axis: there}, device_id_type=MESH,
         )
 
-    def settle_wait(axis, me, n, src, dst, send, recv, hop, k):
-        there = lax.rem(me + k, n)
+    def all_of(axis, me, n, src, dst, send, recv, hop):
         return pltpu.make_async_remote_copy(
-            src_ref=src.at[hop, there], dst_ref=dst.at[hop, there],
-            send_sem=send.at[hop, there], recv_sem=recv.at[hop, there],
-            device_id={axis: there}, device_id_type=MESH,
+            src_ref=src.at[hop, pl.ds(0, n - 1)], dst_ref=dst.at[hop, pl.ds(0, n - 1)],
+            send_sem=send.at[hop], recv_sem=recv.at[hop],
+            device_id={axis: lax.rem(me + 1, n)}, device_id_type=MESH,
         )
 
     AG_U = ("item", me_i, n_item, ag_user, ag_send_u, ag_recv_u)
@@ -126,19 +121,23 @@
         def step(k, carry):
             fn(k)
             return carry
-        lax.fori_loop(1, n, step, 0)
+        if n > 8:
+            lax.fori_loop(1, n, step, 0)
+        else:
+            for k in range(1, n):
+                fn(k)
 
     def start_gather(g, hop):
         each(g[2], lambda k: gather_copy(*g, hop, k).start())
 
     def end_gather(g, hop):
-        each(g[2], lambda k: gather_wait(*g, hop, k).wait_recv())
+        all_of(*g[:4], *g[3:], hop).wait_recv()
 
     def start_settle(s, hop):
         each(s[2], lambda k: settle_copy(*s, hop, k).start())
 
     def end_settle(s, hop):
-        each(s[2], lambda k: settle_wait(*s, hop, k).wait_recv())
+        all_of(*s, hop).wait_recv()
 
     start_gather(AG_U, 0)
     start_gather(AG_I, 0)
@@ -274,10 +273,10 @@
         user_grad[:, whole_lanes:piece_u] = unfold(wire, whole_lanes, grain)
 
     for hop in range(2):
-        each(n_item, lambda k: gather_copy(*AG_U, hop, k).wait_send())
-        each(n_user, lambda k: gather_copy(*AG_I, hop, k).wait_send())
-        each(n_item, lambda k: settle_copy(*RS_U, hop, k).wait_send())
-        each(n_user, lambda k: settle_copy(*RS_I, hop, k).wait_send())
+        for g in (AG_U, AG_I):
+            all_of(*g[:4], *g[3:], hop).wait_send()
+        for s in (RS_U, RS_I):
+            all_of(*s, hop).wait_send()
 
 
 def shards(n_user, n_item, user_cot, item_cot, tile_weight, tile_rows, tile_cols, tile_count, user_degree, item_degree):
@@ -325,8 +324,7 @@
             pltpu.VMEM((2, n_item, *wire_u), sent),
             pltpu.VMEM((2, n_user, *wire_i), sent),
             dma((slots,)), dma((7,)),
-            dma((2, n_item)), dma((2, n_item)), dma((2, n_user)), dma((2, n_user)),
-            dma((2, n_item)), dma((2, n_item)), dma((2, n_user)), dma((2, n_user)),
+            *[dma((2,))] * 8,
         ],
         compiler_params=pltpu.CompilerParams(
             collective_id=0, has_side_effects=True, vmem_limit_bytes=62 * 1024 * 1024

time: 34.6 us -> 33.1 us (0.957)
  Pallas kernels: 30.2 us -> 28.7 us
    pallas_call x1, Pallas kernels: 30.2 us -> 28.7 us  [shards(): pl.pallas_call(functools.partial(kernel, sizes), out_shape=(jax.ShapeDtyp...]
where the time goes in v3:
time: 33.1 us; the launch traced here: 32.9 us
  Pallas kernels  28.7 us (87%)
  local copies, waits for them, and re-layouts  2.85 us (9%)
  between operations  1.29 us (4%)
    pallas_call x1, Pallas kernels, shards(): pl.pallas_call(functools.partial(kernel, sizes), out_shape=(jax.ShapeDtyp...  28.7 us
    unnamed x2, local copies, waits for them, and re-layouts  2.85 us

profile of v3, /device:TPU:0, one launch (start us, length us, event | category | flops | bytes accessed | tf_op | source)
XLA Modules:
  0.0 32.9 jit_solution(6104802754072510499)
XLA Ops:
  1.3 28.7 %shard_map.95 = (bf16[64,192]{1,0:T(8,128)(2,1)}, bf16[64,512]{1,0:T(8,128)(2,1)}) custom-call(bf16[64,192]{1,0:T(8,128)(2,1)} %bitcast.6, bf16[64,512]{1,0:T(8,128)(2,1)} %bitcast.4, s32[16,256,256]{2,1,0:T(8,128)} %weight.1, s32[1,16]{1,0:T(1,128)} %rows_in.1, s32[1,16]{1,0:T(1,128)} %cols_in.1, s32[1,1]{1,0:T(1,128)S(6)} %copy.12.count_in, ...), custom_call_target="tpu_custom_call" | custom-call | tf_op jit(solution)/shard_map/pallas_call | solution.py:294
  30.0 1.4 %copy.13 = bf16[192,64]{0,1:T(8,128)(2,1)} copy(bf16[192,64]{0,1:T(8,128)(2,1)} %bitcast.7) | data formatting | bytes 49152
  31.4 1.5 %copy.14 = bf16[512,64]{0,1:T(8,128)(2,1)} copy(bf16[512,64]{0,1:T(8,128)(2,1)} %bitcast.5) | data formatting | bytes 131072

commit v4 on v3

--- a/solution.py
+++ b/solution.py
@@ -33,11 +33,8 @@
             (rows_in, rows), (cols_in, cols), (count_in, count),
         ])
     ]
-    for copy in small:
+    for copy in small[:2]:
         copy.start()
-    for t in range(slots):
-        pltpu.make_async_copy(weight.at[t], raw.at[t], load_sem.at[t]).start()
-
     barrier = pltpu.get_barrier_semaphore()
 
     def greet(axis, me, n):
@@ -54,6 +51,11 @@
 
     greet("item", me_i, n_item)
     greet("user", me_u, n_user)
+    for copy in small[2:]:
+        copy.start()
+    for t in range(slots):
+        pltpu.make_async_copy(weight.at[t], raw.at[t], load_sem.at[t]).start()
+
 
     grain = math.gcd(piece_u, 128)
     folds, whole_lanes = 128 // grain, piece_u // 128 * 128
@@ -139,8 +141,8 @@
     def end_settle(s, hop):
         all_of(*s, hop).wait_recv()
 
+    start_gather(AG_I, 0)
     start_gather(AG_U, 0)
-    start_gather(AG_I, 0)
 
     for copy in small[2:]:
         copy.wait()
@@ -210,8 +212,8 @@
                 out_user[hop, p, at : at + value.shape[0], :] = value
 
             fold_in(put, lambda lane, size: lanes(p * piece_u + lane, size))
+        start_settle(RS_U, hop)
         in_user[hop, me_i] = out_user[hop, me_i]
-        start_settle(RS_U, hop)
 
     def item_terms(hop):
         end_gather(AG_U, hop)
@@ -237,8 +239,8 @@
             for lane in range(0, tile, 128):
                 p, off = divmod(c * tile + lane, piece_i)
                 out_item[hop, p, :, off : off + 128] = done[:, lane : lane + 128]
+        start_settle(RS_I, hop)
         in_item[hop, me_u] = out_item[hop, me_u]
-        start_settle(RS_I, hop)
 
     def total(s, hop):
         end_settle(s, hop)
@@ -294,8 +296,8 @@
     user_grad, item_grad = pl.pallas_call(
         functools.partial(kernel, sizes),
         out_shape=(
-            jax.ShapeDtypeStruct((width, piece_u), BF16),
-            jax.ShapeDtypeStruct((width, piece_i), BF16),
+            pltpu.VMEM((width, piece_u), BF16),
+            pltpu.VMEM((width, piece_i), BF16),
         ),
         in_specs=[pl.BlockSpec(memory_space=pl.ANY)] * 8,
         out_specs=(vmem, vmem),
@@ -327,7 +329,7 @@
             *[dma((2,))] * 8,
         ],
         compiler_params=pltpu.CompilerParams(
-            collective_id=0, has_side_effects=True, vmem_limit_bytes=62 * 1024 * 1024
+            collective_id=0, has_side_effects=True, vmem_limit_bytes=60 * 1024 * 1024
         ),
     )(
         user_cot.T, item_cot.T, tile_weight, tile_rows, tile_cols, tile_count,

time: 33.1 us -> 30.7 us (0.927)
  local copies, waits for them, and re-layouts: 2.85 us -> 1.25 us
  Pallas kernels: 28.7 us -> 28 us
    unnamed x2, local copies, waits for them, and re-layouts: 2.85 us -> 1.25 us
    pallas_call x1, Pallas kernels: 28.7 us -> 28 us  [shards(): pl.pallas_call(functools.partial(kernel, sizes), out_shape=(pltpu.VMEM((w...]
where the time goes in v4:
time: 30.7 us; the launch traced here: 30.6 us
  Pallas kernels  28 us (91%)
  between operations  1.29 us (4%)
  local copies, waits for them, and re-layouts  1.25 us (4%)
    pallas_call x1, Pallas kernels, shards(): pl.pallas_call(functools.partial(kernel, sizes), out_shape=(pltpu.VMEM((w...  28 us
    unnamed x2, local copies, waits for them, and re-layouts  1.25 us

profile of v4, /device:TPU:0, one launch (start us, length us, event | category | flops | bytes accessed | tf_op | source)
XLA Modules:
  0.0 30.6 jit_solution(14682601473703911131)
XLA Ops:
  1.3 28.0 %shard_map.95 = (bf16[64,192]{1,0:T(8,128)(2,1)S(1)}, bf16[64,512]{1,0:T(8,128)(2,1)S(1)}) custom-call(bf16[64,192]{1,0:T(8,128)(2,1)} %bitcast.7, bf16[64,512]{1,0:T(8,128)(2,1)} %bitcast.6, s32[16,256,256]{2,1,0:T(8,128)} %weight.1, s32[1,16]{1,0:T(1,128)} %rows_in.1, s32[1,16]{1,0:T(1,128)} %cols_in.1, s32[1,1]{1,0:T(1,128)S(6)} %copy.14.count_in, ...), custom_call_target="tpu_custom_call" | custom-call | tf_op jit(solution)/shard_map/pallas_call | solution.py:296
  29.3 0.6 %copy.12 = bf16[192,64]{0,1:T(8,128)(2,1)} copy(bf16[192,64]{0,1:T(8,128)(2,1)S(1)} %bitcast.5) | data formatting | bytes 49152
  29.9 0.6 %copy.13 = bf16[512,64]{0,1:T(8,128)(2,1)} copy(bf16[512,64]{0,1:T(8,128)(2,1)S(1)} %bitcast.4) | data formatting | bytes 131072

commit v5 on v4

--- a/solution.py
+++ b/solution.py
@@ -137,6 +137,17 @@
 
     def start_settle(s, hop):
         each(s[2], lambda k: settle_copy(*s, hop, k).start())
+
+    def send_now(s, hop, p):
+        axis, me, n, src, dst, send, recv = s
+
+        @pl.when(p != me)
+        def _():
+            pltpu.make_async_remote_copy(
+                src_ref=src.at[hop, p], dst_ref=dst.at[hop, me],
+                send_sem=send.at[hop], recv_sem=recv.at[hop],
+                device_id={axis: jnp.int32(p)}, device_id_type=MESH,
+            ).start()
 
     def end_settle(s, hop):
         all_of(*s, hop).wait_recv()
@@ -212,7 +223,7 @@
                 out_user[hop, p, at : at + value.shape[0], :] = value
 
             fold_in(put, lambda lane, size: lanes(p * piece_u + lane, size))
-        start_settle(RS_U, hop)
+            send_now(RS_U, hop, p)
         in_user[hop, me_i] = out_user[hop, me_i]
 
     def item_terms(hop):
@@ -239,7 +250,8 @@
             for lane in range(0, tile, 128):
                 p, off = divmod(c * tile + lane, piece_i)
                 out_item[hop, p, :, off : off + 128] = done[:, lane : lane + 128]
-        start_settle(RS_I, hop)
+                if off + 128 == piece_i:
+                    send_now(RS_I, hop, p)
         in_item[hop, me_u] = out_item[hop, me_u]
 
     def total(s, hop):

time: 30.7 us -> 30.4 us (level)
  no operation moved by 1% of the time
where the time goes in v5:
time: 30.4 us; the launch traced here: 30.3 us
  Pallas kernels  27.7 us (91%)
  between operations  1.29 us (4%)
  local copies, waits for them, and re-layouts  1.25 us (4%)
    pallas_call x1, Pallas kernels, shards(): pl.pallas_call(functools.partial(kernel, sizes), out_shape=(pltpu.VMEM((w...  27.7 us
    unnamed x2, local copies, waits for them, and re-layouts  1.25 us

profile of v5, /device:TPU:0, one launch (start us, length us, event | category | flops | bytes accessed | tf_op | source)
XLA Modules:
  0.0 30.3 jit_solution(4882630762567970161)
XLA Ops:
  1.3 27.7 %shard_map.95 = (bf16[64,192]{1,0:T(8,128)(2,1)S(1)}, bf16[64,512]{1,0:T(8,128)(2,1)S(1)}) custom-call(bf16[64,192]{1,0:T(8,128)(2,1)} %bitcast.7, bf16[64,512]{1,0:T(8,128)(2,1)} %bitcast.6, s32[16,256,256]{2,1,0:T(8,128)} %weight.1, s32[1,16]{1,0:T(1,128)} %rows_in.1, s32[1,16]{1,0:T(1,128)} %cols_in.1, s32[1,1]{1,0:T(1,128)S(6)} %copy.14.count_in, ...), custom_call_target="tpu_custom_call" | custom-call | tf_op jit(solution)/shard_map/pallas_call | solution.py:308
  29.0 0.6 %copy.12 = bf16[192,64]{0,1:T(8,128)(2,1)} copy(bf16[192,64]{0,1:T(8,128)(2,1)S(1)} %bitcast.5) | data formatting | bytes 49152
  29.6 0.6 %copy.13 = bf16[512,64]{0,1:T(8,128)(2,1)} copy(bf16[512,64]{0,1:T(8,128)(2,1)S(1)} %bitcast.4) | data formatting | bytes 131072

commit v6 on v5

--- a/solution.py
+++ b/solution.py
@@ -126,7 +126,7 @@
         if n > 8:
             lax.fori_loop(1, n, step, 0)
         else:
-            for k in range(1, n):
+            for k in [*range(2, n), 1] if n == n_user else range(1, n):
                 fn(k)
 
     def start_gather(g, hop):

time: 30.4 us -> 30.6 us (level)
  no operation moved by 1% of the time
where the time goes in v6:
time: 30.6 us; the launch traced here: 30.5 us
  Pallas kernels  27.9 us (91%)
  between operations  1.29 us (4%)
  local copies, waits for them, and re-layouts  1.25 us (4%)
    pallas_call x1, Pallas kernels, shards(): pl.pallas_call(functools.partial(kernel, sizes), out_shape=(pltpu.VMEM((w...  27.9 us
    unnamed x2, local copies, waits for them, and re-layouts  1.25 us

profile of v6, /device:TPU:0, one launch (start us, length us, event | category | flops | bytes accessed | tf_op | source)
XLA Modules:
  0.0 30.5 jit_solution(2303669379837967368)
XLA Ops:
  1.3 27.9 %shard_map.95 = (bf16[64,192]{1,0:T(8,128)(2,1)S(1)}, bf16[64,512]{1,0:T(8,128)(2,1)S(1)}) custom-call(bf16[64,192]{1,0:T(8,128)(2,1)} %bitcast.7, bf16[64,512]{1,0:T(8,128)(2,1)} %bitcast.6, s32[16,256,256]{2,1,0:T(8,128)} %weight.1, s32[1,16]{1,0:T(1,128)} %rows_in.1, s32[1,16]{1,0:T(1,128)} %cols_in.1, s32[1,1]{1,0:T(1,128)S(6)} %copy.14.count_in, ...), custom_call_target="tpu_custom_call" | custom-call | tf_op jit(solution)/shard_map/pallas_call | solution.py:308
  29.2 0.6 %copy.12 = bf16[192,64]{0,1:T(8,128)(2,1)} copy(bf16[192,64]{0,1:T(8,128)(2,1)S(1)} %bitcast.5) | data formatting | bytes 49152
  29.8 0.6 %copy.13 = bf16[512,64]{0,1:T(8,128)(2,1)} copy(bf16[512,64]{0,1:T(8,128)(2,1)S(1)} %bitcast.4) | data formatting | bytes 131072
